TPU v7x, 32 devices: a whole 2x2x4 slice. The times are simulated.
32 devices in a mesh: corpus: 4 (over y, x), blk: 8 (over z, core).
Axes of the slice: x: 2, y: 2, z: 4, core: 2. Of those that a mesh axis runs over, the one named last changes fastest.
Arguments:
- embedding: bfloat16 [8192, 1024], P(('corpus', 'blk'))
- cluster: int32 [8192], P(('corpus', 'blk')), may hold values from 0 to 7, as said below
- order: int32 [8192], P(('corpus', 'blk')), may hold values from 0 to 8191, each once
Outputs:
- nearest: float32 [8192], P(('corpus', 'blk'))
Inputs may be any that keep to these rules, and one draw needn't show every extreme that they name: On every device, at most 128 documents have clusters with any one value of cluster mod 4. All devices with the same blk index have one common value that exactly 128 of their documents take. `order`: each number appears once.
All inputs are finite; a program needn't handle non-finite values.
Results may differ from a plain program's by a relative error of at most 0.0013.
Values may be sent and summed in bfloat16 or wider, within the bound.
A program may use at most 128 MiB of HBM per device.

v0:
```python
import jax
import jax.numpy as jnp
from jax import lax
from jax.sharding import PartitionSpec as P


def from_behind(block, axis, distance):
    devices = range(lax.axis_size(axis))
    route = [((i - distance) % len(devices), i) for i in devices]
    return lax.ppermute(block, axis, route)


def normalize(values):
    wide = values.astype(jnp.float32)
    return (wide * lax.rsqrt(jnp.sum(wide * wide, axis=1, keepdims=True) + 1e-06)).astype(
        jnp.bfloat16
    )


def similarity(left, right):
    return lax.dot_general(
        left, right, (((1,), (1,)), ((), ())), preferred_element_type=jnp.float32
    )


def local(embedding, cluster, order):
    groups = lax.axis_size("corpus")
    capacity = embedding.shape[0] // 2
    count = groups * capacity
    unit = normalize(embedding)
    target = jnp.mod(cluster, groups)
    picks = (target[:, None] == jnp.arange(groups, dtype=jnp.int32)[None, :]).astype(jnp.int32)
    ranks = jnp.cumsum(picks, axis=0) - 1
    place = target * capacity + jnp.sum(picks * ranks, axis=1)
    send_vecs = jnp.zeros((count, unit.shape[1]), jnp.bfloat16).at[place].set(unit)
    send_keys = jnp.full((count,), -1, jnp.int32).at[place].set(cluster)
    send_order = jnp.zeros((count,), jnp.int32).at[place].set(order)
    got_vecs, got_keys, got_order = (
        lax.all_to_all(
            send_vecs.reshape(groups, capacity, -1),
            "corpus",
            split_axis=0,
            concat_axis=0,
            tiled=True,
        ),
        lax.all_to_all(
            send_keys.reshape(groups, capacity), "corpus", split_axis=0, concat_axis=0, tiled=True
        ),
        lax.all_to_all(
            send_order.reshape(groups, capacity), "corpus", split_axis=0, concat_axis=0, tiled=True
        ),
    )
    vecs = got_vecs.reshape(count, -1)
    keys = got_keys.reshape(count)
    ranks_recv = got_order.reshape(count)
    lowest = jnp.full((count,), -1.0, jnp.float32)
    cycle_size = lax.axis_size("blk")
    here = lax.axis_index("blk")
    sims = similarity(vecs, vecs)
    keep = (
        (keys[:, None] == keys[None, :])
        & (keys[:, None] >= 0)
        & (ranks_recv[None, :] < ranks_recv[:, None])
    )
    best = jnp.maximum(lowest, jnp.max(jnp.where(keep, sims, jnp.float32(-1.0)), axis=1))

    def turn(step, state):
        moving, best_now, columns = state
        moving = from_behind((moving[0], moving[1], moving[2]), "blk", 1)
        sims = similarity(vecs, moving[0])
        same = (keys[:, None] == moving[1][None, :]) & (keys[:, None] >= 0)
        earlier = moving[2][None, :] < ranks_recv[:, None]
        best_now = jnp.maximum(
            best_now, jnp.max(jnp.where(same & earlier, sims, jnp.float32(-1.0)), axis=1)
        )
        later_side = jnp.max(
            jnp.where(same & jnp.logical_not(earlier), sims, jnp.float32(-1.0)), axis=0
        )
        owner_row = jnp.mod(here - step, cycle_size)
        columns = lax.dynamic_update_slice(columns, later_side[None, :], (owner_row, jnp.int32(0)))
        return (moving, best_now, columns)

    start_cols = jnp.full((cycle_size, count), -1.0, jnp.float32)
    unused, best, columns = lax.fori_loop(
        1, cycle_size // 2 + 1, turn, ((vecs, keys, ranks_recv), best, start_cols)
    )
    returned = lax.all_to_all(columns, "blk", split_axis=0, concat_axis=0, tiled=True)
    best = jnp.maximum(best, jnp.max(returned, axis=0))
    back = lax.all_to_all(
        best.reshape(groups, capacity), "corpus", split_axis=0, concat_axis=0, tiled=True
    )
    return back.reshape(-1)[place]


def solution(mesh):
    in_specs = (P(("corpus", "blk"), None), P(("corpus", "blk")), P(("corpus", "blk")))
    out_specs = P(("corpus", "blk"))
    return jax.shard_map(local, mesh=mesh, in_specs=in_specs, out_specs=out_specs, check_vma=False)
```

profile of v0, /device:TPU:0, one launch (start us, length us, event | category | flops | bytes accessed | tf_op | source)
XLA Modules:
  0.0 126.5 jit_solution(15523119161298837969)
XLA Ops:
  0.0 0.8 fusion.19
  0.8 1.2 reduce-window.6
  2.0 0.1 slice.10
  2.1 0.1 copy.8
  2.2 0.1 copy.9
  2.3 0.1 add_bitcast_fusion
  2.4 2.0 %scatter_custom_fusion.1 = s32[512]{0:T(512)} fusion(s32[256]{0:T(256)S(1)} %compare_select_fusion, s32[256]{0:T(256)S(1)} %copy-done.1, s32[]{:T(128)} %constant.107.clone.1), kind=kCustom, calls=%fused_computation.36 | custom fusion | bytes 2052 | tf_op jit(solution)/shard_map/scatter | solution.py:36
  4.4 5.2 %all-to-all-start.1 = ((s32[4,1,128]{2,1,0:T(1,128)}), s32[4,1,128]{2,1,0:T(1,128)S(1)}, u32[]{:S(2)}, u32[]{:S(2)}) async-start(s32[4,1,128]{2,1,0:T(1,128)} %bitcast.8), calls=%async_computation.1 | async-start | bytes 4096 | tf_op jit(solution)/shard_map/all_to_all | solution.py:46
  9.6 1.2 fusion.2
  10.8 2.1 %scatter_custom_fusion.2 = s32[512]{0:T(512)} fusion(s32[256]{0:T(256)S(1)} %compare_select_fusion, s32[256]{0:T(256)} %param.7, s32[]{:T(128)} %constant.102.clone.1), kind=kCustom, calls=%fused_computation.34 | custom fusion | bytes 2560 | tf_op jit(solution)/shard_map/scatter | solution.py:37
  12.9 1.1 all-to-all-done.1
  14.1 3.2 %all-to-all-start.2 = ((s32[4,1,128]{2,1,0:T(1,128)}), s32[4,1,128]{2,1,0:T(1,128)S(1)}, u32[]{:S(2)}, u32[]{:S(2)}) async-start(s32[4,1,128]{2,1,0:T(1,128)} %bitcast.10), calls=%async_computation.2 | async-start | bytes 4096 | tf_op jit(solution)/shard_map/all_to_all | solution.py:49
  17.3 2.7 %scatter_custom_fusion = bf16[512,1024]{1,0:T(8,128)(2,1)} fusion(s32[256]{0:T(256)S(1)} %compare_select_fusion, bf16[256,1024]{1,0:T(8,128)(2,1)S(1)} %copy-done, f32[256]{0:T(256)S(1)} %add_rsqrt_fusion, bf16[]{:T(256)} %constant.103.clone.1), kind=kCustom, calls=%fused_computation.17 | custom fusion | flops 786432 | bytes 1573890 | tf_op jit(solution)/shard_map/scatter | solution.py:35
  20.1 1.7 %all-to-all-done.2 = s32[4,1,128]{2,1,0:T(1,128)S(1)} async-done(((s32[4,1,128]{2,1,0:T(1,128)}), s32[4,1,128]{2,1,0:T(1,128)S(1)}, u32[]{:S(2)}, u32[]{:S(2)}) %all-to-all-start.2) | async-done | bytes 2080 | tf_op jit(solution)/shard_map/all_to_all | solution.py:49
  21.8 3.5 %all-to-all-start = ((bf16[4,128,1024]{2,1,0:T(8,128)(2,1)}), bf16[4,128,1024]{2,1,0:T(8,128)(2,1)S(1)}, u32[]{:S(2)}, u32[]{:S(2)}) async-start(bf16[4,128,1024]{2,1,0:T(8,128)(2,1)} %bitcast.6), calls=%async_computation | async-start | bytes 2097152 | tf_op jit(solution)/shard_map/all_to_all | solution.py:39
  25.3 11.8 %all-to-all-done = bf16[4,128,1024]{2,1,0:T(8,128)(2,1)S(1)} async-done(((bf16[4,128,1024]{2,1,0:T(8,128)(2,1)}), bf16[4,128,1024]{2,1,0:T(8,128)(2,1)S(1)}, u32[]{:S(2)}, u32[]{:S(2)}) %all-to-all-start) | async-done | bytes 1048608 | tf_op jit(solution)/shard_map/all_to_all | solution.py:39
  37.2 0.1 copy.14
  37.3 0.9 fusion.1
  38.1 69.4 %while.23 = (s32[]{:T(128)}, bf16[512,1024]{1,0:T(8,128)(2,1)S(1)}, s32[512]{0:T(512)S(1)}, s32[512]{0:T(512)S(1)}, f32[512]{0:T(512)S(1)}, /*index=5*/f32[8,512...) while((s32[]{:T(128)}, bf16[512,1024]{1,0:T(8,128)(2,1)S(1)}, ...), condition=%wide.region_11.12_spmd, body=%wide.region_8.11_spmd.sunk | while | flops 539492352 | bytes 8439196 | solution.py:84
  38.2 0.1 collective-permute-start
  38.2 1.7 %collective-permute-start.1 = (s32[512]{0:T(512)S(1)}, s32[512]{0:T(512)S(1)}, u32[]{:S(2)}, u32[]{:S(2)}) collective-permute-start(s32[512]{0:T(512)S(1)} %get-tuple-element.354), channel_id=1, source_target_pairs={{7,0},{0,1},{1,2},{2,3},{3,4},{4,5},{5,6},{6,7},{15,8},{8,9},{9,10... | collective-permute-start | bytes 6152 | tf_op jit(solution)/shard_map/while/body/eval_jaxpr/ppermute | solution.py:10
  39.9 0.1 collective-permute-start.2
  40.0 14.3 %collective-permute-done.1 = s32[512]{0:T(512)S(1)} collective-permute-done((s32[512]{0:T(512)S(1)}, s32[512]{0:T(512)S(1)}, u32[]{:S(2)}, u32[]{:S(2)}) %collective-permute-start.1) | collective-permute-done | bytes 2080 | tf_op jit(solution)/shard_map/while/body/eval_jaxpr/ppermute | solution.py:10
  54.3 1.1 select_reduce_fusion.3
  55.4 0.1 dynamic_update_slice.11
  55.4 0.1 copy.26
  55.5 0.1 collective-permute-start
  55.6 0.1 collective-permute-start.1
  55.6 0.1 collective-permute-start.2
  55.8 15.9 %collective-permute-done.1 = s32[512]{0:T(512)S(1)} collective-permute-done((s32[512]{0:T(512)S(1)}, s32[512]{0:T(512)S(1)}, u32[]{:S(2)}, u32[]{:S(2)}) %collective-permute-start.1) | collective-permute-done | bytes 2080 | tf_op jit(solution)/shard_map/while/body/eval_jaxpr/ppermute | solution.py:10
  71.6 1.1 select_reduce_fusion.3
  72.7 0.1 dynamic_update_slice.11
  72.8 0.1 copy.26
  72.9 0.1 collective-permute-start
  72.9 0.1 collective-permute-start.1
  73.1 15.9 %collective-permute-done.1 = s32[512]{0:T(512)S(1)} collective-permute-done((s32[512]{0:T(512)S(1)}, s32[512]{0:T(512)S(1)}, u32[]{:S(2)}, u32[]{:S(2)}) %collective-permute-start.1) | collective-permute-done | bytes 2080 | tf_op jit(solution)/shard_map/while/body/eval_jaxpr/ppermute | solution.py:10
  89.0 1.1 select_reduce_fusion.3
  90.1 0.1 dynamic_update_slice.11
  90.1 0.1 copy.26
  90.5 15.9 %collective-permute-done.1 = s32[512]{0:T(512)S(1)} collective-permute-done((s32[512]{0:T(512)S(1)}, s32[512]{0:T(512)S(1)}, u32[]{:S(2)}, u32[]{:S(2)}) %collective-permute-start.1) | collective-permute-done | bytes 2080 | tf_op jit(solution)/shard_map/while/body/eval_jaxpr/ppermute | solution.py:10
  106.3 1.1 select_reduce_fusion.3
  107.4 0.1 dynamic_update_slice.11
  107.5 0.1 copy.26
  107.6 8.0 %all_to_all.47 = f32[8,1,512]{2,1,0:T(1,128)S(1)} all-to-all(f32[8,1,512]{2,1,0:T(1,128)S(1)} %all_to_all.38), channel_id=1, replica_groups=mesh['corpus'=4,'blk'=8] {'blk'}, dimensions={0} | all-to-all | bytes 32768 | tf_op jit(solution)/shard_map/all_to_all | solution.py:87
  115.6 0.6 max.13
  116.2 3.2 %all-to-all-start.4 = ((f32[4,1,128]{2,1,0:T(1,128)}), f32[4,1,128]{2,1,0:T(1,128)S(1)}, u32[]{:S(2)}, u32[]{:S(2)}) async-start(f32[4,1,128]{2,1,0:T(1,128)} %bitcast.14), calls=%async_computation.4 | async-start | bytes 4096 | tf_op jit(solution)/shard_map/all_to_all | solution.py:89
  119.5 4.4 %all-to-all-done.4 = f32[4,1,128]{2,1,0:T(1,128)S(1)} async-done(((f32[4,1,128]{2,1,0:T(1,128)}), f32[4,1,128]{2,1,0:T(1,128)S(1)}, u32[]{:S(2)}, u32[]{:S(2)}) %all-to-all-start.4) | async-done | bytes 2080 | tf_op jit(solution)/shard_map/all_to_all | solution.py:89
  124.0 2.5 %gather_fusion = f32[256]{0:T(256)} fusion(f32[512]{0:T(512)S(1)} %bitcast.47, s32[1024]{0:T(1024)S(1)} %pad_clamp_fusion), kind=kCustom, calls=%fused_computation | custom fusion | bytes 3072 | tf_op jit(solution)/shard_map/gather | solution.py:92
  (47 shorter events, 0.6 us)
Async XLA Ops:
  0.0 0.8 copy-start.1
  0.0 17.3 %copy-start = (bf16[256,1024]{1,0:T(8,128)(2,1)S(1)}, bf16[256,1024]{1,0:T(8,128)(2,1)}, u32[]{:S(2)}) copy-start(bf16[256,1024]{1,0:T(8,128)(2,1)} %param.5) | copy-start | bytes 1572868
  4.4 9.7 %all-to-all-start.1 = ((s32[4,1,128]{2,1,0:T(1,128)}), s32[4,1,128]{2,1,0:T(1,128)S(1)}, u32[]{:S(2)}, u32[]{:S(2)}) async-start(s32[4,1,128]{2,1,0:T(1,128)} %bitcast.8), calls=%async_computation.1 | async-start | bytes 4096 | tf_op jit(solution)/shard_map/all_to_all | solution.py:46
  14.1 7.7 %all-to-all-start.2 = ((s32[4,1,128]{2,1,0:T(1,128)}), s32[4,1,128]{2,1,0:T(1,128)S(1)}, u32[]{:S(2)}, u32[]{:S(2)}) async-start(s32[4,1,128]{2,1,0:T(1,128)} %bitcast.10), calls=%async_computation.2 | async-start | bytes 4096 | tf_op jit(solution)/shard_map/all_to_all | solution.py:49
  21.8 15.4 %all-to-all-start = ((bf16[4,128,1024]{2,1,0:T(8,128)(2,1)}), bf16[4,128,1024]{2,1,0:T(8,128)(2,1)S(1)}, u32[]{:S(2)}, u32[]{:S(2)}) async-start(bf16[4,128,1024]{2,1,0:T(8,128)(2,1)} %bitcast.6), calls=%async_computation | async-start | bytes 2097152 | tf_op jit(solution)/shard_map/all_to_all | solution.py:39
  38.2 16.1 %collective-permute-start = (bf16[512,1024]{1,0:T(8,128)(2,1)S(1)}, bf16[512,1024]{1,0:T(8,128)(2,1)S(1)}, u32[]{:S(2)}, u32[]{:S(2)}) collective-permute-start(bf16[512,1024]{1,0:T(8,128)(2,1)S(1)} %get-tuple-element.353), channel_id=1, source_target_pairs={{7,0},{0,1},{1,2},{2,3},{3,4},{4,5},{5,6},{6,7},{15,8},{8,9},{9,10... | collective-permute-start | bytes 3145736 | tf_op jit(solution)/shard_map/while/body/eval_jaxpr/ppermute | solution.py:10
  38.2 16.0 %collective-permute-start.1 = (s32[512]{0:T(512)S(1)}, s32[512]{0:T(512)S(1)}, u32[]{:S(2)}, u32[]{:S(2)}) collective-permute-start(s32[512]{0:T(512)S(1)} %get-tuple-element.354), channel_id=1, source_target_pairs={{7,0},{0,1},{1,2},{2,3},{3,4},{4,5},{5,6},{6,7},{15,8},{8,9},{9,10... | collective-permute-start | bytes 6152 | tf_op jit(solution)/shard_map/while/body/eval_jaxpr/ppermute | solution.py:10
  39.9 14.4 %collective-permute-start.2 = (s32[512]{0:T(512)S(1)}, s32[512]{0:T(512)S(1)}, u32[]{:S(2)}, u32[]{:S(2)}) collective-permute-start(s32[512]{0:T(512)S(1)} %get-tuple-element.355), channel_id=1, source_target_pairs={{7,0},{0,1},{1,2},{2,3},{3,4},{4,5},{5,6},{6,7},{15,8},{8,9},{9,10... | collective-permute-start | bytes 6152 | tf_op jit(solution)/shard_map/while/body/eval_jaxpr/ppermute | solution.py:10
  55.5 16.1 %collective-permute-start = (bf16[512,1024]{1,0:T(8,128)(2,1)S(1)}, bf16[512,1024]{1,0:T(8,128)(2,1)S(1)}, u32[]{:S(2)}, u32[]{:S(2)}) collective-permute-start(bf16[512,1024]{1,0:T(8,128)(2,1)S(1)} %get-tuple-element.353), channel_id=1, source_target_pairs={{7,0},{0,1},{1,2},{2,3},{3,4},{4,5},{5,6},{6,7},{15,8},{8,9},{9,10... | collective-permute-start | bytes 3145736 | tf_op jit(solution)/shard_map/while/body/eval_jaxpr/ppermute | solution.py:10
  55.6 16.0 %collective-permute-start.1 = (s32[512]{0:T(512)S(1)}, s32[512]{0:T(512)S(1)}, u32[]{:S(2)}, u32[]{:S(2)}) collective-permute-start(s32[512]{0:T(512)S(1)} %get-tuple-element.354), channel_id=1, source_target_pairs={{7,0},{0,1},{1,2},{2,3},{3,4},{4,5},{5,6},{6,7},{15,8},{8,9},{9,10... | collective-permute-start | bytes 6152 | tf_op jit(solution)/shard_map/while/body/eval_jaxpr/ppermute | solution.py:10
  55.6 16.0 %collective-permute-start.2 = (s32[512]{0:T(512)S(1)}, s32[512]{0:T(512)S(1)}, u32[]{:S(2)}, u32[]{:S(2)}) collective-permute-start(s32[512]{0:T(512)S(1)} %get-tuple-element.355), channel_id=1, source_target_pairs={{7,0},{0,1},{1,2},{2,3},{3,4},{4,5},{5,6},{6,7},{15,8},{8,9},{9,10... | collective-permute-start | bytes 6152 | tf_op jit(solution)/shard_map/while/body/eval_jaxpr/ppermute | solution.py:10
  72.9 16.1 %collective-permute-start = (bf16[512,1024]{1,0:T(8,128)(2,1)S(1)}, bf16[512,1024]{1,0:T(8,128)(2,1)S(1)}, u32[]{:S(2)}, u32[]{:S(2)}) collective-permute-start(bf16[512,1024]{1,0:T(8,128)(2,1)S(1)} %get-tuple-element.353), channel_id=1, source_target_pairs={{7,0},{0,1},{1,2},{2,3},{3,4},{4,5},{5,6},{6,7},{15,8},{8,9},{9,10... | collective-permute-start | bytes 3145736 | tf_op jit(solution)/shard_map/while/body/eval_jaxpr/ppermute | solution.py:10
  72.9 16.0 %collective-permute-start.1 = (s32[512]{0:T(512)S(1)}, s32[512]{0:T(512)S(1)}, u32[]{:S(2)}, u32[]{:S(2)}) collective-permute-start(s32[512]{0:T(512)S(1)} %get-tuple-element.354), channel_id=1, source_target_pairs={{7,0},{0,1},{1,2},{2,3},{3,4},{4,5},{5,6},{6,7},{15,8},{8,9},{9,10... | collective-permute-start | bytes 6152 | tf_op jit(solution)/shard_map/while/body/eval_jaxpr/ppermute | solution.py:10
  73.0 16.0 %collective-permute-start.2 = (s32[512]{0:T(512)S(1)}, s32[512]{0:T(512)S(1)}, u32[]{:S(2)}, u32[]{:S(2)}) collective-permute-start(s32[512]{0:T(512)S(1)} %get-tuple-element.355), channel_id=1, source_target_pairs={{7,0},{0,1},{1,2},{2,3},{3,4},{4,5},{5,6},{6,7},{15,8},{8,9},{9,10... | collective-permute-start | bytes 6152 | tf_op jit(solution)/shard_map/while/body/eval_jaxpr/ppermute | solution.py:10
  90.2 16.1 %collective-permute-start = (bf16[512,1024]{1,0:T(8,128)(2,1)S(1)}, bf16[512,1024]{1,0:T(8,128)(2,1)S(1)}, u32[]{:S(2)}, u32[]{:S(2)}) collective-permute-start(bf16[512,1024]{1,0:T(8,128)(2,1)S(1)} %get-tuple-element.353), channel_id=1, source_target_pairs={{7,0},{0,1},{1,2},{2,3},{3,4},{4,5},{5,6},{6,7},{15,8},{8,9},{9,10... | collective-permute-start | bytes 3145736 | tf_op jit(solution)/shard_map/while/body/eval_jaxpr/ppermute | solution.py:10
  90.3 16.0 %collective-permute-start.1 = (s32[512]{0:T(512)S(1)}, s32[512]{0:T(512)S(1)}, u32[]{:S(2)}, u32[]{:S(2)}) collective-permute-start(s32[512]{0:T(512)S(1)} %get-tuple-element.354), channel_id=1, source_target_pairs={{7,0},{0,1},{1,2},{2,3},{3,4},{4,5},{5,6},{6,7},{15,8},{8,9},{9,10... | collective-permute-start | bytes 6152 | tf_op jit(solution)/shard_map/while/body/eval_jaxpr/ppermute | solution.py:10
  90.4 16.0 %collective-permute-start.2 = (s32[512]{0:T(512)S(1)}, s32[512]{0:T(512)S(1)}, u32[]{:S(2)}, u32[]{:S(2)}) collective-permute-start(s32[512]{0:T(512)S(1)} %get-tuple-element.355), channel_id=1, source_target_pairs={{7,0},{0,1},{1,2},{2,3},{3,4},{4,5},{5,6},{6,7},{15,8},{8,9},{9,10... | collective-permute-start | bytes 6152 | tf_op jit(solution)/shard_map/while/body/eval_jaxpr/ppermute | solution.py:10
  116.2 7.7 %all-to-all-start.4 = ((f32[4,1,128]{2,1,0:T(1,128)}), f32[4,1,128]{2,1,0:T(1,128)S(1)}, u32[]{:S(2)}, u32[]{:S(2)}) async-start(f32[4,1,128]{2,1,0:T(1,128)} %bitcast.14), calls=%async_computation.4 | async-start | bytes 4096 | tf_op jit(solution)/shard_map/all_to_all | solution.py:89
where the time goes:
time: 127 us; the launch traced here: 126 us
  waiting for transfers between devices  81.1 us (64%)
  starting transfers between devices  17.5 us (14%)
  blocking collectives  8.02 us (6%)
  local copies, waits for them, and re-layouts  7.5 us (6%)
  other arithmetic  6.81 us (5%)
  matrix products  5.1 us (4%)
    ppermute x12, waiting for transfers between devices, from_behind(): return lax.ppermute(block, axis, route)  61.9 us
    all_to_all x1, waiting for transfers between devices, local(): lax.all_to_all(send_vecs.reshape(groups, capacity, -1), 'corpus', split_a...  11.8 us
    all_to_all x1, blocking collectives, local(): lax.all_to_all(columns, 'blk', split_axis=0, concat_axis=0, tiled=True)  8.02 us
    all_to_all x1, starting transfers between devices, local(): lax.all_to_all(send_keys.reshape(groups, capacity), 'corpus', split_axis=...  5.16 us
    dot_general x5, matrix products, similarity(): lax.dot_general(left, right, (((1,), (1,)), ((), ())), preferred_element_...  5.1 us
    all_to_all x1, waiting for transfers between devices, local(): lax.all_to_all(best.reshape(groups, capacity), 'corpus', split_axis=0, co...  4.45 us
    all_to_all x1, starting transfers between devices, local(): lax.all_to_all(send_vecs.reshape(groups, capacity, -1), 'corpus', split_a...  3.52 us
    all_to_all x1, starting transfers between devices, local(): lax.all_to_all(best.reshape(groups, capacity), 'corpus', split_axis=0, co...  3.24 us
  transfers between devices with their start and end apart: 16, of which 8 were waited for; matrix products, arithmetic and copies ran while one was open for 5% of the time, Pallas kernels for 0%

commit v1 on v0

v1 whole, which is shorter than its diff:
```python
import functools

import jax
import jax.numpy as jnp
from jax import lax
from jax.experimental import pallas as pl
from jax.experimental.pallas import tpu as pltpu
from jax.sharding import PartitionSpec as P

CORES = 2
CHUNKS = 2


def flip(value, mask, bits):
    out = 0
    for b in range(bits):
        bit = lax.rem(lax.div(value, 1 << b), 2)
        if mask >> b & 1:
            bit = 1 - bit
        out = out + bit * (1 << b)
    return out


def popcount(d):
    return bin(d).count("1")


def kernel(
    groups,
    places,
    emb_ref,
    clus_ref,
    ord_ref,
    out_ref,
    rows,
    cols,
    rmeta,
    cmeta,
    rclus,
    rord,
    rowacc,
    ownacc,
    colres,
    rowres,
    gotrow,
    gotcol,
    rows_send,
    rows_recv,
    sib_send,
    sib_recv,
    cols_send,
    cols_recv,
    rmeta_send,
    rmeta_recv,
    cmeta_send,
    cmeta_recv,
    rres_send,
    rres_recv,
    cres_send,
    cres_recv,
):
    docs = emb_ref.shape[0]
    part = docs // CHUNKS
    bits = groups.bit_length() - 1
    half = places // 2
    even = places % 2 == 0
    c = lax.axis_index("corpus")
    b = lax.axis_index("blk")
    p = lax.div(b, CORES)
    k = lax.rem(b, CORES)

    def plane(d, j):
        return {"corpus": flip(c, d, bits), "blk": p * CORES + (k if j == 0 else 1 - k)}

    def along(s):
        return {"corpus": c, "blk": lax.rem(p + s + places, places) * CORES + k}

    def meets(position, s):
        if even and s == half:
            return position >= places - half
        return None

    def when(cond, f):
        if cond is None:
            f()
        else:
            pl.when(cond)(f)

    def remote(src, dst, send, recv, device):
        return pltpu.make_async_remote_copy(
            src_ref=src,
            dst_ref=dst,
            send_sem=send,
            recv_sem=recv,
            device_id=device,
            device_id_type=pl.DeviceIdType.MESH,
        )

    def piece(ref, i, t):
        return ref.at[i, pl.ds(t * part, part), :]

    plane_peers = [(d, j) for d in range(groups) for j in range(2) if (d, j) != (0, 0)]
    barrier = pltpu.get_barrier_semaphore()
    for d, j in plane_peers:
        pl.semaphore_signal(barrier, inc=1, device_id=plane(d, j), device_id_type=pl.DeviceIdType.MESH)
    for s in range(1, places):
        pl.semaphore_signal(barrier, inc=1, device_id=along(s), device_id_type=pl.DeviceIdType.MESH)

    def normalise(t):
        wide = emb_ref[pl.ds(t * part, part), :].astype(jnp.float32)
        scale = lax.rsqrt(jnp.sum(wide * wide, axis=1, keepdims=True) + 1e-06)
        rows[0, pl.ds(t * part, part), :] = (wide * scale).astype(jnp.bfloat16)

    def col_copy(s, t):
        src = piece(rows, 0, t) if s == 1 else piece(cols, s - 2, t)
        return remote(src, piece(cols, s - 1, t), cols_send.at[s - 1, t], cols_recv.at[s - 1, t], along(1))

    def col_send(s, t):
        when(meets(lax.rem(p + 1, places), s), lambda: col_copy(s, t).start())

    def via(d, t):
        ones = [1 << i for i in range(bits) if d >> i & 1]
        return ones[t % len(ones)]

    def row_copy(d, t):
        hop = via(d, t)
        return remote(
            piece(rows, 2 * (d ^ hop), t),
            piece(rows, 2 * d, t),
            rows_send.at[d, t],
            rows_recv.at[d, t],
            plane(hop, 0),
        )

    def sib_copy(d, t):
        return remote(
            piece(rows, 2 * d, t), piece(rows, 2 * d + 1, t), sib_send.at[d, t], sib_recv.at[d, t], plane(0, 1)
        )

    def order_of(d):
        first = 0 if d & 1 == 0 else 1
        return [(first + t) % CHUNKS for t in range(CHUNKS)]

    normalise(0)
    rmeta[0] = jnp.concatenate(
        [clus_ref[...], ord_ref[...], jnp.zeros((6, docs), jnp.int32)], axis=0
    ).astype(jnp.float32)
    pl.semaphore_wait(barrier, len(plane_peers) + places - 1)

    singles = [1 << i for i in range(bits)]
    metas = []
    for t in range(CHUNKS):
        if t:
            normalise(t)
        if places > 1:
            col_send(1, t)
        for d in singles:
            if t == order_of(d)[0]:
                row_copy(d, t).start()
        if t == 0:
            for s in range(1, half + 1):
                cp = remote(rmeta.at[0], cmeta.at[s - 1], cmeta_send.at[s - 1], cmeta_recv.at[s - 1], along(s))
                when(meets(lax.rem(p + s, places), s), cp.start)
            for d, j in plane_peers:
                i = 2 * d + j
                cp = remote(rmeta.at[0], rmeta.at[i], rmeta_send.at[i], rmeta_recv.at[i], plane(d, j))
                cp.start()
                metas.append(cp)
        sib_copy(0, t).start()
    for i in range(1, CHUNKS):
        for d in singles:
            row_copy(d, order_of(d)[i]).start()

    def spread(i):
        for row, ref in ((0, rclus), (1, rord)):
            line = jnp.broadcast_to(rmeta[i, row : row + 1, :], (128, docs))
            ref[pl.ds(i * docs, docs), :] = line.T

    spread(0)
    rowacc[...] = jnp.full(rowacc.shape, -1.0, jnp.float32)
    colres[...] = jnp.full(colres.shape, -1.0, jnp.float32)
    ownacc[...] = jnp.full(ownacc.shape, -1.0, jnp.float32)

    def similar(left, right):
        return lax.dot_general(left, right, (((1,), (1,)), ((), ())), preferred_element_type=jnp.float32)

    def fold(x):
        return jnp.max(x.reshape(x.shape[0] // 8, 8, x.shape[1]), axis=0)

    def with_self(i):
        sims = similar(rows[i], rows[0])
        for t in range(docs // 128):
            lanes = slice(t * 128, (t + 1) * 128)
            at = pl.ds(i * docs, docs)
            keep = (rclus[at, :] == rmeta[0, 0:1, lanes]) & (rord[at, :] < rmeta[0, 1:2, lanes])
            ownacc[:, lanes] = jnp.maximum(ownacc[:, lanes], fold(jnp.where(keep, sims[:, lanes], -1.0)))

    def cross(s, t, i):
        lanes = slice(t * part, (t + 1) * part)
        sims = similar(rows[i], cols[s - 1, lanes, :])
        at = pl.ds(pl.multiple_of(i * docs, docs), docs)
        same = jnp.where(rclus[at, :] == cmeta[s - 1, 0:1, lanes], sims, -1.0)
        earlier = cmeta[s - 1, 1:2, lanes] < rord[at, :]
        rowacc[at, :] = jnp.maximum(rowacc[at, :], jnp.where(earlier, same, -1.0))
        colres[s - 1, :, lanes] = jnp.maximum(
            colres[s - 1, :, lanes], fold(jnp.where(earlier, -1.0, same))
        )

    def cross_all(s, t, ds):
        slots = [2 * d + j for d in ds for j in range(2)]
        if slots == list(range(slots[0], slots[0] + len(slots))) and len(slots) > 2:

            @pl.loop(0, len(slots) // 2)
            def _(n):
                cross(s, t, slots[0] + 2 * n)
                cross(s, t, slots[0] + 2 * n + 1)
        else:
            for i in slots:
                cross(s, t, i)

    def wait_cols(s, t):
        col_copy(s, t).wait_recv()
        if s < half:
            col_send(s + 1, t)

    sent_cols = []

    def return_cols(s):
        cp = remote(colres.at[s - 1], gotcol.at[s - 1], cres_send.at[s - 1], cres_recv.at[s - 1], along(-s))
        cp.start()

    rounds = max(bits, half)
    for r in range(rounds + 1):
        now = [d for d in range(groups) if popcount(d) == r]
        here = [d for d in range(groups) if popcount(d) <= r]
        before = [d for d in range(groups) if popcount(d) < r]
        for i in range(CHUNKS):
            if r:
                for d in now:
                    t = order_of(d)[i]
                    row_copy(d, t).wait_recv()
                    for e in range(groups):
                        if popcount(e) == r + 1 and e ^ via(e, t) == d:
                            row_copy(e, t).start()
                    sib_copy(d, t).start()
            if 1 <= r < half:
                wait_cols(r, i)
        if r == 0:
            with_self(0)
            for cp in metas:
                cp.wait_recv()
            for i in range(1, 2 * groups):
                spread(i)
        for d in now:
            for t in range(CHUNKS):
                sib_copy(d, t).wait_recv()
            if r:
                with_self(2 * d)
            with_self(2 * d + 1)
        for s in range(1, min(r, half + 1)):
            if now:

                def older(s=s):
                    for t in range(CHUNKS):
                        cross_all(s, t, now)

                when(meets(p, s), older)
        if 1 <= r <= half:

            def newest(s=r):
                remote(
                    rmeta.at[0], cmeta.at[s - 1], cmeta_send.at[s - 1], cmeta_recv.at[s - 1], along(s)
                ).wait_recv()
                for t in range(CHUNKS):
                    if s >= half:
                        wait_cols(s, t)
                    cross_all(s, t, here)

            when(meets(p, r), newest)
        for s in range(1, half + 1):
            if r == max(s, bits):
                when(meets(p, s), functools.partial(return_cols, s))

    finals = []
    for d in range(groups):
        for j in range(2):
            i = 2 * d + j
            rowres[i] = fold(rowacc[pl.ds(i * docs, docs), :].T)
            if i:
                cp = remote(rowres.at[i], gotrow.at[i], rres_send.at[i], rres_recv.at[i], plane(d, j))
                cp.start()
                finals.append(cp)

    ownacc[...] = jnp.maximum(ownacc[...], rowres[0])
    for s in range(1, half + 1):

        def take(s=s):
            remote(
                colres.at[s - 1], gotcol.at[s - 1], cres_send.at[s - 1], cres_recv.at[s - 1], along(-s)
            ).wait_recv()
            ownacc[...] = jnp.maximum(ownacc[...], gotcol[s - 1])

        when(meets(lax.rem(p + s, places), s), take)
    for i, cp in enumerate(finals):
        cp.wait_recv()
        ownacc[...] = jnp.maximum(ownacc[...], gotrow[i + 1])
    out_ref[...] = jnp.max(ownacc[...], axis=0, keepdims=True)

    for cp in metas + finals:
        cp.wait_send()
    for t in range(CHUNKS):
        for d in range(groups):
            if d:
                row_copy(d, t).wait_send()
            sib_copy(d, t).wait_send()
    for s in range(1, half + 1):

        def sent(s=s):
            for t in range(CHUNKS):
                col_copy(s, t).wait_send()

        def sent_meta(s=s):
            remote(
                rmeta.at[0], cmeta.at[s - 1], cmeta_send.at[s - 1], cmeta_recv.at[s - 1], along(s)
            ).wait_send()

        def sent_back(s=s):
            remote(
                colres.at[s - 1], gotcol.at[s - 1], cres_send.at[s - 1], cres_recv.at[s - 1], along(-s)
            ).wait_send()

        when(meets(lax.rem(p + 1, places), s), sent)
        when(meets(lax.rem(p + s, places), s), sent_meta)
        when(meets(p, s), sent_back)


def local(groups, places, embedding, cluster, order):
    docs, width = embedding.shape
    half = places // 2
    slots = 2 * groups
    dma = pltpu.SemaphoreType.DMA
    out = pl.pallas_call(
        functools.partial(kernel, groups, places),
        out_shape=jax.ShapeDtypeStruct((1, docs), jnp.float32),
        in_specs=[pl.BlockSpec(memory_space=pltpu.VMEM)] * 3,
        out_specs=pl.BlockSpec(memory_space=pltpu.VMEM),
        scratch_shapes=[
            pltpu.VMEM((slots, docs, width), jnp.bfloat16),
            pltpu.VMEM((half, docs, width), jnp.bfloat16),
            pltpu.VMEM((slots, 8, docs), jnp.float32),
            pltpu.VMEM((half, 8, docs), jnp.float32),
            pltpu.VMEM((slots * docs, 128), jnp.float32),
            pltpu.VMEM((slots * docs, 128), jnp.float32),
            pltpu.VMEM((slots * docs, 128), jnp.float32),
            pltpu.VMEM((8, docs), jnp.float32),
            pltpu.VMEM((half, 8, docs), jnp.float32),
            pltpu.VMEM((slots, 8, docs), jnp.float32),
            pltpu.VMEM((slots, 8, docs), jnp.float32),
            pltpu.VMEM((half, 8, docs), jnp.float32),
            dma((groups, CHUNKS)),
            dma((groups, CHUNKS)),
            dma((groups, CHUNKS)),
            dma((groups, CHUNKS)),
            dma((half, CHUNKS)),
            dma((half, CHUNKS)),
            dma((slots,)),
            dma((slots,)),
            dma((half,)),
            dma((half,)),
            dma((slots,)),
            dma((slots,)),
            dma((half,)),
            dma((half,)),
        ],
        compiler_params=pltpu.CompilerParams(
            collective_id=0, has_side_effects=True, vmem_limit_bytes=40 * 2**20
        ),
    )(embedding, cluster.reshape(1, docs), order.reshape(1, docs))
    return out.reshape(docs)


def solution(mesh):
    body = functools.partial(local, mesh.shape["corpus"], mesh.shape["blk"] // CORES)
    in_specs = (P(("corpus", "blk"), None), P(("corpus", "blk")), P(("corpus", "blk")))
    out_specs = P(("corpus", "blk"))
    return jax.shard_map(body, mesh=mesh, in_specs=in_specs, out_specs=out_specs, check_vma=False)
```

time: 127 us -> 37.7 us (0.30)
  waiting for transfers between devices: 81.1 us -> 0 us
  Pallas kernels: 0 us -> 35.2 us
  starting transfers between devices: 17.5 us -> 0 us
  blocking collectives: 8.02 us -> 0 us
  other arithmetic: 6.81 us -> 0 us
  local copies, waits for them, and re-layouts: 7.5 us -> 2.3 us
  matrix products: 5.1 us -> 0 us
    ppermute x12 -> x0, waiting for transfers between devices: 61.9 us -> none  [from_behind(): return lax.ppermute(block, axis, route)]
    pallas_call x0 -> x1, Pallas kernels: none -> 35.2 us  [local(): pl.pallas_call(functools.partial(kernel, groups, places), out_shape=jax.S...]
    all_to_all x4 -> x0, waiting for transfers between devices: 19.1 us -> none  [the longest x1 11.8 us: local(): lax.all_to_all(send_vecs.reshape(groups, capacity, -1), 'corpus', split_a...]
    all_to_all x4 -> x0, starting transfers between devices: 15.2 us -> none  [the longest x1 5.16 us: local(): lax.all_to_all(send_keys.reshape(groups, capacity), 'corpus', split_axis=...]
    all_to_all x1 -> x0, blocking collectives: 8.02 us -> none  [local(): lax.all_to_all(columns, 'blk', split_axis=0, concat_axis=0, tiled=True)]
    dot_general x5 -> x0, matrix products: 5.1 us -> none  [similarity(): lax.dot_general(left, right, (((1,), (1,)), ((), ())), preferred_element_...]
    scatter x2 -> x0, local copies, waits for them, and re-layouts: 4.09 us -> none  [the longest x1 2.12 us: local(): send_order = jnp.zeros((count,), jnp.int32).at[place].set(order)]
    scatter x1 -> x0, other arithmetic: 2.73 us -> none  [local(): jnp.zeros((count, unit.shape[1]), jnp.bfloat16).at[place].set(unit)]
  transfers between devices with their start and end apart: 16 -> 0, of which waited for: 8 -> 0; matrix products, arithmetic and copies ran while one was open for 5% -> 0% of each run, Pallas kernels for 0% -> 0%
where the time goes in v1:
time: 37.7 us; the launch traced here: 37.5 us
  Pallas kernels  35.2 us (93%)
  local copies, waits for them, and re-layouts  2.3 us (6%)
    pallas_call x1, Pallas kernels, local(): pl.pallas_call(functools.partial(kernel, groups, places), out_shape=jax.S...  35.2 us
    unnamed x7, local copies, waits for them, and re-layouts  2.3 us

profile of v1, /device:TPU:0, one launch (start us, length us, event | category | flops | bytes accessed | tf_op | source)
XLA Modules:
  0.0 37.5 jit_solution(4895367710260811589)
XLA Ops:
  0.0 0.0 copy-start.2
  0.0 0.0 copy-start.1
  0.0 0.7 %copy-done.2 = s32[256]{0:T(256)S(1)} copy-done((s32[256]{0:T(256)S(1)}, s32[256]{0:T(256)}, u32[]{:S(2)}) %copy-start.2) | copy-done | bytes 1048
  0.7 0.0 copy-done.1
  0.7 0.0 copy-start
  0.7 1.0 %copy-done = bf16[256,1024]{1,0:T(8,128)(2,1)S(1)} copy-done((bf16[256,1024]{1,0:T(8,128)(2,1)S(1)}, bf16[256,1024]{1,0:T(8,128)(2,1)}, u32[]{:S(2)}) %copy-start) | copy-done | bytes 524312
  1.7 35.2 %shard_map.37 = f32[1,256]{1,0:T(1,128)S(1)} custom-call(bf16[256,1024]{1,0:T(8,128)(2,1)S(1)} %copy-done, s32[1,256]{1,0:T(1,128)S(1)} %bitcast.4, s32[1,256]{1,0:T(1,128)S(1)} %bitcast.5), custom_call_target="tpu_custom_call" | custom-call | tf_op jit(solution)/shard_map/pallas_call | solution.py:342
  37.0 0.6 %copy.5 = f32[256]{0:T(256)} copy(f32[256]{0:T(256)S(1)} %bitcast.3) | data formatting | bytes 2048
Async XLA Ops:
  0.0 0.7 %copy-start.2 = (s32[256]{0:T(256)S(1)}, s32[256]{0:T(256)}, u32[]{:S(2)}) copy-start(s32[256]{0:T(256)} %param.5) | copy-start | bytes 3076
  0.0 0.7 %copy-start.1 = (s32[256]{0:T(256)S(1)}, s32[256]{0:T(256)}, u32[]{:S(2)}) copy-start(s32[256]{0:T(256)} %param.4) | copy-start | bytes 3076
  0.7 1.0 %copy-start = (bf16[256,1024]{1,0:T(8,128)(2,1)S(1)}, bf16[256,1024]{1,0:T(8,128)(2,1)}, u32[]{:S(2)}) copy-start(bf16[256,1024]{1,0:T(8,128)(2,1)} %emb_ref.1) | copy-start | bytes 1572868
